TPU v7x, 32 devices: a whole 2x2x4 slice. The times are simulated.
32 devices in a mesh: src: 8 (over z, x), tgt: 4 (over y, core).
Axes of the slice: x: 2, y: 2, z: 4, core: 2. Of those that a mesh axis runs over, the one named last changes fastest.
Arguments:
- sources: float32 [50, 4096], P(None, 'src'), may hold values from -1.2 to 1.2
- targets: float32 [50, 16384], P(None, 'tgt'), may hold values from -1.2 to 1.2
- pair_active: int32 [8, 4], P('src', 'tgt'), may hold values from 0 to 1, as said below
- count_src: int32 [8], replicated, may hold values from 256 to 512, as said below
- count_tgt: int32 [4], replicated, may hold values from 2048 to 4096, as said below
Outputs:
- source_potential: float32 [4096], P('src')
- target_potential: float32 [16384], P('tgt')
- ancestors: float32 [50, 16384], P(None, ('tgt', 'src'))
Inputs may be any that keep to these rules, and one draw needn't show every extreme that they name: `pair_active`: every source block has at least one listed tile and every target tile is listed with at least one source block. `count_src`: some block holds exactly 512 live cells and another exactly 256. `count_tgt`: some tile holds exactly 4096 live cells and another exactly 2048.
All inputs are finite; a program needn't handle non-finite values.
Results may differ from a plain program's by a relative error of at most 0.0003.
Values sent between devices are 32-bit elements; how exact they have to be, the bound alone decides.
No kernel may reach another device: no remote copies, remote signals or barrier semaphores. Data moves between devices by JAX's collectives and lax.ppermute only.
A program may use at most 64 MiB of HBM per device.

v0:
```python
import jax
import jax.numpy as jnp
from jax import lax
from jax.sharding import PartitionSpec as P

ITERS = 4


EPS = 0.02
NEG = -1e30


def shards(sources, targets, pair_active, count_src, count_tgt):
    rows = sources.shape[1]
    cols = targets.shape[1]
    tiles_dev = pair_active.shape[1]
    tile = cols // tiles_dev
    src_index = lax.axis_index("src")
    tgt_index = lax.axis_index("tgt")
    log_a = -jnp.log(jnp.sum(count_src).astype(jnp.float32))
    log_b = -jnp.log(jnp.sum(count_tgt).astype(jnp.float32))
    row_live = jnp.arange(rows, dtype=jnp.int32) < count_src[src_index]
    tile_counts = lax.dynamic_slice_in_dim(count_tgt, tgt_index * tiles_dev, tiles_dev)
    within = jnp.arange(cols, dtype=jnp.int32) % tile
    col_live = within < jnp.repeat(tile_counts, tile)
    col_listed = col_live & jnp.repeat(pair_active[0] > 0, tile)
    allowed = row_live[:, None] & col_listed[None, :]
    left = jnp.sum(sources * sources, axis=0)
    right = jnp.sum(targets * targets, axis=0)
    cross = lax.dot_general(
        sources, targets, (((0,), (0,)), ((), ())), precision=lax.Precision.HIGHEST
    )
    cost = left[:, None] + right[None, :] - 2.0 * cross
    g = jnp.zeros((cols,), jnp.float32)
    f = jnp.zeros((rows,), jnp.float32)
    for step in range(ITERS):
        logits = jnp.where(allowed, (g[None, :] - cost) / EPS, NEG)
        peak = jnp.max(logits, axis=1)
        total = jnp.sum(jnp.where(allowed, jnp.exp(logits - peak[:, None]), 0.0), axis=1)
        best = lax.pmax(peak, "tgt")
        total = lax.psum(total * jnp.exp(peak - best), "tgt")
        peak = best
        f = jnp.where(
            row_live, EPS * (log_a - peak - jnp.log(jnp.where(row_live, total, 1.0))), 0.0
        )
        logits = jnp.where(allowed, (f[:, None] - cost) / EPS, NEG)
        peak = jnp.max(logits, axis=0)
        total = jnp.sum(jnp.where(allowed, jnp.exp(logits - peak[None, :]), 0.0), axis=0)
        best = lax.pmax(peak, "src")
        total = lax.psum(total * jnp.exp(peak - best), "src")
        peak = best
        g = jnp.where(
            col_live, EPS * (log_b - peak - jnp.log(jnp.where(col_live, total, 1.0))), 0.0
        )
    expo = jnp.where(allowed, (f[:, None] + g[None, :] - cost) / EPS - log_b, NEG)
    weight = jnp.where(allowed, jnp.exp(expo), 0.0)
    share = cols // lax.axis_size("src")
    whole = jnp.dot(sources, weight, precision=lax.Precision.HIGHEST)
    summed = lax.psum(whole, "src")
    ancestors = lax.dynamic_slice_in_dim(summed, src_index * share, share, 1)
    return (f, g, ancestors)


def solution(mesh):
    return jax.shard_map(
        shards,
        mesh=mesh,
        in_specs=(P(None, "src"), P(None, "tgt"), P("src", "tgt"), P(), P()),
        out_specs=(P("src"), P("tgt"), P(None, ("tgt", "src"))),
        check_vma=False,
    )
```

profile of v0, /device:TPU:0, one launch (start us, length us, event | category | flops | bytes accessed | tf_op | source)
XLA Modules:
  0.0 521.9 jit_solution(8405361892672970854)
XLA Ops:
  17.1 12.3 %fusion.14 = (f32[512]{0:T(512)S(1)}, f32[512,4096]{1,0:T(8,128)}) fusion(pred[4096]{0:T(1024)(128)(4,1)S(1)} %fusion.35, pred[512]{0:T(512)(128)(4,1)S(1)} %iota_compare_fusion, f32[50,512]{1,0:T(8,128)} %param.5, f32[50,4096]{1,0:T(8,128)} %param.6, f32[4096]{0:T(1024)S(1)} %multiply_reduce_fusion, f32[512]{0:T(512)S(1)} %multiply_reduce_fusion.1), kind=kOutput, calls=%fused_computation.33 | convolution fusion | flops 1275067904 | bytes 9335296 | tf_op jit(solution)/shard_map/dot_general | solution.py:30
  29.4 8.3 %pmax.56 = f32[512]{0:T(512)S(1)} all-reduce(f32[512]{0:T(512)S(1)} %get-tuple-element.3), channel_id=1, replica_groups=mesh['src'=8,'tgt'=4] {'tgt'}, use_global_device_ids=true, to_apply=%region_5.6 | all-reduce | flops 512 | bytes 4096 | tf_op jit(solution)/shard_map/pmax | solution.py:40
  37.8 5.2 %fusion = f32[512]{0:T(512)S(1)} fusion(f32[512,4096]{1,0:T(8,128)} %get-tuple-element.4, f32[512]{0:T(512)S(1)} %get-tuple-element.3, pred[4096]{0:T(1024)(128)(4,1)S(1)} %fusion.35, pred[512]{0:T(512)(128)(4,1)S(1)} %iota_compare_fusion), kind=kLoop, calls=%fused_computation.18 | loop fusion | flops 14679552 | bytes 8397312 | tf_op jit(solution)/shard_map/reduce_sum | solution.py:39
  43.0 5.8 %psum.63 = f32[512]{0:T(512)S(1)} all-reduce(f32[512]{0:T(512)S(1)} %exponential_multiply_fusion.7), channel_id=1, replica_groups=mesh['src'=8,'tgt'=4] {'tgt'}, use_global_device_ids=true, to_apply=%region_7.8 | all-reduce | flops 512 | bytes 4096 | tf_op jit(solution)/shard_map/psum | solution.py:41
  49.4 4.4 fusion.15
  53.9 5.3 %fusion.1 = f32[4096]{0:T(1024)S(1)} fusion(f32[512,4096]{1,0:T(8,128)} %get-tuple-element.4, f32[4096]{0:T(1024)S(1)} %fusion.15, f32[512]{0:T(512)S(1)} %multiply_select_fusion.7, pred[4096]{0:T(1024)(128)(4,1)S(1)} %fusion.35, pred[512]{0:T(512)(128)(4,1)S(1)} %iota_compare_fusion), kind=kLoop, calls=%fused_computation.19 | loop fusion | flops 14675968 | bytes 8428032 | tf_op jit(solution)/shard_map/reduce_sum | solution.py:48
  59.2 37.5 %pmax.57 = f32[4096]{0:T(1024)S(1)} all-reduce(f32[4096]{0:T(1024)S(1)} %fusion.15), channel_id=1, replica_groups=mesh['src'=8,'tgt'=4] {'src'}, use_global_device_ids=true, to_apply=%region_9.10 | all-reduce | flops 4096 | bytes 32768 | tf_op jit(solution)/shard_map/pmax | solution.py:49
  97.3 33.2 %psum.64 = f32[4096]{0:T(1024)S(1)} all-reduce(f32[4096]{0:T(1024)S(1)} %exponential_multiply_fusion.3), channel_id=1, replica_groups=mesh['src'=8,'tgt'=4] {'src'}, use_global_device_ids=true, to_apply=%region_11.12 | all-reduce | flops 4096 | bytes 32768 | tf_op jit(solution)/shard_map/psum | solution.py:50
  131.1 4.5 fusion.16
  135.6 5.4 %fusion.2 = f32[512]{0:T(512)S(1)} fusion(f32[512,4096]{1,0:T(8,128)} %get-tuple-element.4, f32[512]{0:T(512)S(1)} %fusion.16, f32[4096]{0:T(1024)S(1)} %multiply_select_fusion.3, pred[4096]{0:T(1024)(128)(4,1)S(1)} %fusion.35, pred[512]{0:T(512)(128)(4,1)S(1)} %iota_compare_fusion), kind=kLoop, calls=%fused_computation.20 | loop fusion | flops 14679552 | bytes 8413696 | tf_op jit(solution)/shard_map/reduce_sum | solution.py:39
  141.0 5.8 %pmax.58 = f32[512]{0:T(512)S(1)} all-reduce(f32[512]{0:T(512)S(1)} %fusion.16), channel_id=1, replica_groups=mesh['src'=8,'tgt'=4] {'tgt'}, use_global_device_ids=true, to_apply=%region_13.14 | all-reduce | flops 512 | bytes 4096 | tf_op jit(solution)/shard_map/pmax | solution.py:40
  146.8 5.8 %psum.65 = f32[512]{0:T(512)S(1)} all-reduce(f32[512]{0:T(512)S(1)} %exponential_multiply_fusion.6), channel_id=1, replica_groups=mesh['src'=8,'tgt'=4] {'tgt'}, use_global_device_ids=true, to_apply=%region_15.16 | all-reduce | flops 512 | bytes 4096 | tf_op jit(solution)/shard_map/psum | solution.py:41
  157.6 5.3 %fusion.3 = f32[4096]{0:T(1024)S(1)} fusion(f32[512,4096]{1,0:T(8,128)} %get-tuple-element.4, f32[4096]{0:T(1024)S(1)} %fusion.17, f32[512]{0:T(512)S(1)} %multiply_select_fusion.6, pred[4096]{0:T(1024)(128)(4,1)S(1)} %fusion.35, pred[512]{0:T(512)(128)(4,1)S(1)} %iota_compare_fusion), kind=kLoop, calls=%fused_computation.21 | loop fusion | flops 14675968 | bytes 8428032 | tf_op jit(solution)/shard_map/reduce_sum | solution.py:48
  162.9 33.0 %pmax.59 = f32[4096]{0:T(1024)S(1)} all-reduce(f32[4096]{0:T(1024)S(1)} %fusion.17), channel_id=1, replica_groups=mesh['src'=8,'tgt'=4] {'src'}, use_global_device_ids=true, to_apply=%region_17.18 | all-reduce | flops 4096 | bytes 32768 | tf_op jit(solution)/shard_map/pmax | solution.py:49
  195.9 33.0 %psum.66 = f32[4096]{0:T(1024)S(1)} all-reduce(f32[4096]{0:T(1024)S(1)} %exponential_multiply_fusion.2), channel_id=1, replica_groups=mesh['src'=8,'tgt'=4] {'src'}, use_global_device_ids=true, to_apply=%region_19.20 | all-reduce | flops 4096 | bytes 32768 | tf_op jit(solution)/shard_map/psum | solution.py:50
  229.6 4.5 fusion.18
  234.1 5.4 %fusion.4 = f32[512]{0:T(512)S(1)} fusion(f32[512,4096]{1,0:T(8,128)} %get-tuple-element.4, f32[512]{0:T(512)S(1)} %fusion.18, f32[4096]{0:T(1024)S(1)} %multiply_select_fusion.2, pred[4096]{0:T(1024)(128)(4,1)S(1)} %fusion.35, pred[512]{0:T(512)(128)(4,1)S(1)} %iota_compare_fusion), kind=kLoop, calls=%fused_computation.22 | loop fusion | flops 14679552 | bytes 8413696 | tf_op jit(solution)/shard_map/reduce_sum | solution.py:39
  239.5 5.7 %pmax.60 = f32[512]{0:T(512)S(1)} all-reduce(f32[512]{0:T(512)S(1)} %fusion.18), channel_id=1, replica_groups=mesh['src'=8,'tgt'=4] {'tgt'}, use_global_device_ids=true, to_apply=%region_21.22 | all-reduce | flops 512 | bytes 4096 | tf_op jit(solution)/shard_map/pmax | solution.py:40
  245.1 7.0 %psum.67 = f32[512]{0:T(512)S(1)} all-reduce(f32[512]{0:T(512)S(1)} %exponential_multiply_fusion.5), channel_id=1, replica_groups=mesh['src'=8,'tgt'=4] {'tgt'}, use_global_device_ids=true, to_apply=%region_23.24 | all-reduce | flops 512 | bytes 4096 | tf_op jit(solution)/shard_map/psum | solution.py:41
  257.2 5.3 %fusion.5 = f32[4096]{0:T(1024)S(1)} fusion(f32[512,4096]{1,0:T(8,128)} %get-tuple-element.4, f32[4096]{0:T(1024)S(1)} %fusion.19, f32[512]{0:T(512)S(1)} %multiply_select_fusion.5, pred[4096]{0:T(1024)(128)(4,1)S(1)} %fusion.35, pred[512]{0:T(512)(128)(4,1)S(1)} %iota_compare_fusion), kind=kLoop, calls=%fused_computation.23 | loop fusion | flops 14675968 | bytes 8428032 | tf_op jit(solution)/shard_map/reduce_sum | solution.py:48
  262.5 33.0 %pmax.61 = f32[4096]{0:T(1024)S(1)} all-reduce(f32[4096]{0:T(1024)S(1)} %fusion.19), channel_id=1, replica_groups=mesh['src'=8,'tgt'=4] {'src'}, use_global_device_ids=true, to_apply=%region_25.26 | all-reduce | flops 4096 | bytes 32768 | tf_op jit(solution)/shard_map/pmax | solution.py:49
  295.5 33.0 %psum.68 = f32[4096]{0:T(1024)S(1)} all-reduce(f32[4096]{0:T(1024)S(1)} %exponential_multiply_fusion.1), channel_id=1, replica_groups=mesh['src'=8,'tgt'=4] {'src'}, use_global_device_ids=true, to_apply=%region_27.28 | all-reduce | flops 4096 | bytes 32768 | tf_op jit(solution)/shard_map/psum | solution.py:50
  329.1 4.5 fusion.20
  333.6 5.4 %fusion.6 = f32[512]{0:T(512)S(1)} fusion(f32[512,4096]{1,0:T(8,128)} %get-tuple-element.4, f32[512]{0:T(512)S(1)} %fusion.20, f32[4096]{0:T(1024)S(1)} %multiply_select_fusion.1, pred[4096]{0:T(1024)(128)(4,1)S(1)} %fusion.35, pred[512]{0:T(512)(128)(4,1)S(1)} %iota_compare_fusion), kind=kLoop, calls=%fused_computation.24 | loop fusion | flops 14679552 | bytes 8413696 | tf_op jit(solution)/shard_map/reduce_sum | solution.py:39
  339.0 5.7 %pmax.62 = f32[512]{0:T(512)S(1)} all-reduce(f32[512]{0:T(512)S(1)} %fusion.20), channel_id=1, replica_groups=mesh['src'=8,'tgt'=4] {'tgt'}, use_global_device_ids=true, to_apply=%region_29.30 | all-reduce | flops 512 | bytes 4096 | tf_op jit(solution)/shard_map/pmax | solution.py:40
  344.7 6.0 %psum.69 = f32[512]{0:T(512)S(1)} all-reduce(f32[512]{0:T(512)S(1)} %exponential_multiply_fusion.4), channel_id=1, replica_groups=mesh['src'=8,'tgt'=4] {'tgt'}, use_global_device_ids=true, to_apply=%region_31.32 | all-reduce | flops 512 | bytes 4096 | tf_op jit(solution)/shard_map/psum | solution.py:41
  351.4 4.5 fusion.21
  355.9 33.0 %pmax.63 = f32[4096]{0:T(1024)S(1)} all-reduce(f32[4096]{0:T(1024)S(1)} %fusion.21), channel_id=1, replica_groups=mesh['src'=8,'tgt'=4] {'src'}, use_global_device_ids=true, to_apply=%region_33.34 | all-reduce | flops 4096 | bytes 32768 | tf_op jit(solution)/shard_map/pmax | solution.py:49
  388.9 5.3 %fusion.7 = f32[4096]{0:T(1024)S(1)} fusion(f32[512,4096]{1,0:T(8,128)} %get-tuple-element.4, f32[4096]{0:T(1024)S(1)} %fusion.21, f32[512]{0:T(512)S(1)} %multiply_select_fusion.4, pred[4096]{0:T(1024)(128)(4,1)S(1)} %fusion.35, pred[512]{0:T(512)(128)(4,1)S(1)} %iota_compare_fusion), kind=kLoop, calls=%fused_computation.25 | loop fusion | flops 14675968 | bytes 8428032 | tf_op jit(solution)/shard_map/reduce_sum | solution.py:48
  394.2 33.2 %psum.70 = f32[4096]{0:T(1024)S(1)} all-reduce(f32[4096]{0:T(1024)S(1)} %exponential_multiply_fusion), channel_id=1, replica_groups=mesh['src'=8,'tgt'=4] {'src'}, use_global_device_ids=true, to_apply=%region_35.36 | all-reduce | flops 4096 | bytes 32768 | tf_op jit(solution)/shard_map/psum | solution.py:50
  428.1 11.6 %fusion.22 = f32[50,4096]{1,0:T(8,128)} fusion(f32[50,512]{1,0:T(8,128)S(1)} %copy-done, f32[512,4096]{1,0:T(8,128)} %get-tuple-element.4, f32[]{:T(128)S(6)} %neg.7, f32[4096]{0:T(1024)S(1)} %multiply_select_fusion, f32[512]{0:T(512)S(1)} %multiply_select_fusion.4, pred[4096]{0:T(1024)(128)(4,1)S(1)} %fusion.35, pred[512]{0:T(512)(128)(4,1)S(1)} %iota_compare_fusion), kind=kOutput, calls=%fused_computation.41 | convolution fusion | flops 1272971264 | bytes 9333252 | tf_op jit(solution)/shard_map/dot_general | solution.py:58
  439.8 73.7 %all-reduce.2.cloned.1.call-done = f32[50,4096]{1,0:T(8,128)} async-done(((f32[50,4096]{1,0:T(8,128)}), f32[50,4096]{1,0:T(8,128)}) %all-reduce.2.cloned.1.call-update) | async-done | bytes 819216 | tf_op jit(solution)/shard_map/psum | solution.py:59
  (35 shorter events, 24.4 us)
Async XLA Ops:
  7.2 506.3 %all-reduce.2.cloned.1.call-start = ((), (), s32[]{:S(2)}) async-start(), calls=%async_computation | async-start | bytes 1835008 | tf_op jit(solution)/shard_map/psum | solution.py:59
  351.4 76.7 %copy-start.1 = (f32[512]{0:T(512)}, f32[512]{0:T(512)S(1)}, u32[]{:S(2)}) copy-start(f32[512]{0:T(512)S(1)} %multiply_select_fusion.4) | copy-start | bytes 6148
  351.4 76.7 %copy-start = (f32[50,512]{1,0:T(8,128)S(1)}, f32[50,512]{1,0:T(8,128)}, u32[]{:S(2)}) copy-start(f32[50,512]{1,0:T(8,128)} %param.5) | copy-start | bytes 307204
  428.1 11.7 %copy-start.2 = (f32[4096]{0:T(1024)}, f32[4096]{0:T(1024)S(1)}, u32[]{:S(2)}) copy-start(f32[4096]{0:T(1024)S(1)} %multiply_select_fusion) | copy-start | bytes 49156
Sparse Core Ops, SparseCore 0:
  439.9 73.5 all-reduce.1
where the time goes:
time: 523 us; the launch traced here: 522 us
  blocking collectives  319 us (61%)
  other arithmetic  85.2 us (16%)
  waiting for transfers between devices  73.7 us (14%)
  matrix products  23.9 us (5%)
  between operations  16.2 us (3%)
    pmax x4, blocking collectives, shards(): best = lax.pmax(peak, 'src')  136 us
    psum x4, blocking collectives, shards(): total = lax.psum(total * jnp.exp(peak - best), 'src')  132 us
    psum x1, waiting for transfers between devices, shards(): summed = lax.psum(whole, 'src')  73.7 us
    pmax x4, blocking collectives, shards(): best = lax.pmax(peak, 'tgt')  25.4 us
    psum x4, blocking collectives, shards(): total = lax.psum(total * jnp.exp(peak - best), 'tgt')  24.5 us
    reduce_sum x4, other arithmetic, shards(): jnp.sum(jnp.where(allowed, jnp.exp(logits - peak[:, None]), 0.0), axis=1)  21.4 us
    reduce_sum x4, other arithmetic, shards(): jnp.sum(jnp.where(allowed, jnp.exp(logits - peak[None, :]), 0.0), axis=0)  21.1 us
    reduce_max x4, other arithmetic, shards(): peak = jnp.max(logits, axis=0)  17.8 us
  transfers between devices with their start and end apart: 1, of which 1 were waited for; matrix products, arithmetic and copies ran while one was open for 0% of the time, Pallas kernels for 0%

commit v1 on v0

v1 whole, which is shorter than its diff:
```python
import functools
import math

import jax
import jax.numpy as jnp
from jax import lax
from jax.experimental import pallas as pl
from jax.experimental.pallas import tpu as pltpu
from jax.sharding import PartitionSpec as P

ITERS = 4
EPS = 0.02
NEG = -1e30
LOG2E = math.log2(math.e)
SCALE = LOG2E / EPS
LANES = 128
DEPTH = 64
VMEM_LIMIT = 40 * 1024 * 1024

VMEM_SPEC = pl.BlockSpec(memory_space=pltpu.VMEM)
SMEM_SPEC = pl.BlockSpec(memory_space=pltpu.SMEM)


def pinned(x):
    return pltpu.with_memory_space_constraint(x, pltpu.VMEM)


def split(x):
    high = x.astype(jnp.bfloat16)
    rest = x - high.astype(jnp.float32)
    mid = rest.astype(jnp.bfloat16)
    low = (rest - mid.astype(jnp.float32)).astype(jnp.bfloat16)
    return high, mid, low


def to_sublanes(row_ref, col_ref, size):
    for start in range(0, size, LANES):
        piece = jnp.broadcast_to(row_ref[0:1, start : start + LANES], (LANES, LANES))
        col_ref[start : start + LANES, :] = piece.T


def fold_lanes(peak_ref, total_ref):
    peaks = peak_ref[...].T
    top = jnp.max(peaks, axis=0, keepdims=True)
    total = jnp.sum(total_ref[...].T * jnp.exp2(peaks - top), axis=0, keepdims=True)
    return top + jnp.log2(total)


def row_lse(score_ref, add_ref, peak_ref, total_ref, out_ref):
    rows, cols = score_ref.shape

    def block(i, _):
        here = pl.ds(pl.multiple_of(i * 8, 8), 8)
        z = []
        for start in range(0, cols, LANES):
            lanes = slice(start, start + LANES)
            value = score_ref[here, lanes]
            if add_ref is not None:
                value = value + add_ref[0:1, lanes]
            z.append(value)
        peak = functools.reduce(jnp.maximum, z)
        total = functools.reduce(jnp.add, [jnp.exp2(v - peak) for v in z])
        peak_ref[here, :] = peak
        total_ref[here, :] = total
        return 0

    lax.fori_loop(0, rows // 8, block, 0, unroll=2)
    out_ref[...] = fold_lanes(peak_ref, total_ref)


def col_lse(score_ref, add_ref, out_ref):
    rows, cols = score_ref.shape
    wide = 4

    def block(c, _):
        tops = [jnp.full((8, LANES), -jnp.inf, jnp.float32)] * wide
        spots = [pl.ds(pl.multiple_of((c * wide + k) * LANES, LANES), LANES) for k in range(wide)]
        for r in range(0, rows, 8):
            add = add_ref[r : r + 8, :]
            tops = [jnp.maximum(t, score_ref[r : r + 8, s] + add) for t, s in zip(tops, spots)]
        peaks = [jnp.broadcast_to(jnp.max(t, axis=0, keepdims=True), (8, LANES)) for t in tops]
        sums = [jnp.zeros((8, LANES), jnp.float32)] * wide
        for r in range(0, rows, 8):
            add = add_ref[r : r + 8, :]
            sums = [u + jnp.exp2(score_ref[r : r + 8, s] + (add - p)) for u, s, p in zip(sums, spots, peaks)]
        for s, p, u in zip(spots, peaks, sums):
            out_ref[0:1, s] = p[0:1] + jnp.log2(jnp.sum(u, axis=0, keepdims=True))
        return 0

    lax.fori_loop(0, cols // (LANES * wide), block, 0)


def transposed_terms(left):
    high, mid, low = split(left.T)
    return jnp.concatenate([high, high, mid, mid, high, low], axis=1)


def right_terms(right):
    high, mid, low = split(right)
    return jnp.concatenate([high, mid, high, mid, low, high], axis=0)


def pad_into(pad_ref, values):
    pad_ref[...] = jnp.zeros(pad_ref.shape, jnp.float32)
    pad_ref[0 : values.shape[0], :] = values


def live_sum(counts):
    total = counts[0]
    for i in range(1, counts.shape[0]):
        total = total + counts[i]
    return jnp.full((1, LANES), total, jnp.int32).astype(jnp.float32)


def wide(x, size):
    return jnp.concatenate([x] * (size // LANES), axis=1)


def first_kernel(
    src_hbm, tgt_hbm, count_src_hbm, count_tgt_hbm, pair,
    score_ref, lse_ref, row_aux, col_aux, own_ref, half_ref, token_ref,
    src_ref, tgt_ref, count_src, count_tgt, sems,
    right_pad, left_pad, own_pad, terms_ref, norm_ref, col_ref, peak_ref, total_ref,
):
    rows, cols = score_ref.shape
    dims = src_ref.shape[0]
    copies = [
        pltpu.make_async_copy(one, two, sems.at[i])
        for i, (one, two) in enumerate(
            [(count_src_hbm, count_src), (count_tgt_hbm, count_tgt), (src_hbm, src_ref), (tgt_hbm, tgt_ref)]
        )
    ]
    for copy in copies:
        copy.start()
    for ref in (right_pad, left_pad, own_pad, token_ref):
        ref[...] = jnp.zeros(ref.shape, jnp.float32)
    half = DEPTH // 2
    mine = pl.ds(pl.multiple_of((lax.axis_index("tgt") % 2) * half, half), half)
    theirs = pl.ds(pl.multiple_of((1 - lax.axis_index("tgt") % 2) * half, half), half)
    for copy in copies[:3]:
        copy.wait()
    n_rows = count_src[lax.axis_index("src")]
    n_cols = count_tgt[lax.axis_index("tgt")]
    listed = pair[0, 0] > 0
    row_live = lax.broadcasted_iota(jnp.int32, (1, rows), 1) < n_rows
    col_live = lax.broadcasted_iota(jnp.int32, (1, cols), 1) < n_cols
    row_aux[0:1, :] = row_live.astype(jnp.float32)
    row_aux[1:2, :] = jnp.where(row_live, wide(-jnp.log2(live_sum(count_src)), rows), 0.0)
    row_aux[2:3, :] = (row_live & listed).astype(jnp.float32)
    col_aux[0:1, :] = col_live.astype(jnp.float32)
    col_aux[1:2, :] = jnp.where(col_live, wide(-jnp.log2(live_sum(count_tgt)), cols), 0.0)
    left_pad[0:dims, :] = src_ref[...]
    half_ref[0] = left_pad[mine, :]
    left = left_pad[...]
    norm_ref[0:1, :] = jnp.where(row_live, -SCALE * jnp.sum(left * left, axis=0, keepdims=True), NEG)
    to_sublanes(norm_ref, col_ref, rows)
    terms_ref[...] = transposed_terms(left * (2.0 * SCALE))
    copies[3].wait()
    size = 512

    def block(c, _):
        here = pl.ds(pl.multiple_of(c * size, size), size)
        right_pad[0:dims, :] = tgt_ref[:, here]
        right = right_pad[...]
        spot = lax.broadcasted_iota(jnp.int32, (1, size), 1) + c * size
        norm = -SCALE * jnp.sum(right * right, axis=0, keepdims=True)
        norm = jnp.where((spot < n_cols) & listed, norm, NEG)
        cross = jnp.dot(terms_ref[...], right_terms(right), preferred_element_type=jnp.float32)
        score_ref[:, here] = cross + (wide(col_ref[...], size) + norm)
        return 0

    lax.fori_loop(0, cols // size, block, 0)
    share = own_ref.shape[1]
    own_pad[0:dims, :] = tgt_ref[:, pl.ds(pl.multiple_of(lax.axis_index("src") * share, share), share)]
    own_ref[0:half, :] = own_pad[mine, :]
    own_ref[half:, :] = own_pad[theirs, :]
    row_lse(score_ref, None, peak_ref, total_ref, lse_ref)


def slab_kernel(own_ref, mine_ref, theirs_ref, slab_ref, token_ref, right_pad, terms_ref, norm_ref, col_ref, *, first):
    share = own_ref.shape[1]
    _, half, rows = mine_ref.shape
    left = own_ref[...]
    norm_ref[0:1, :] = -SCALE * jnp.sum(left * left, axis=0, keepdims=True)
    to_sublanes(norm_ref, col_ref, share)
    terms_ref[...] = transposed_terms(left * (2.0 * SCALE))
    for b in range(slab_ref.shape[1] // rows):
        right_pad[0:half, :] = mine_ref[first + b]
        right_pad[half:, :] = theirs_ref[first + b]
        right = right_pad[...]
        norm = -SCALE * jnp.sum(right * right, axis=0, keepdims=True)
        cross = jnp.dot(terms_ref[...], right_terms(right), preferred_element_type=jnp.float32)
        slab_ref[:, b * rows : (b + 1) * rows] = cross + (wide(col_ref[...], rows) + norm)
    token_ref[...] = jnp.zeros(token_ref.shape, jnp.float32)


def col_kernel(score_ref, lse_ref, aux_ref, out_ref, f_ref, masked_ref, col_ref):
    f = aux_ref[1:2, :] - lse_ref[...] * aux_ref[0:1, :]
    f_ref[...] = f
    masked_ref[...] = jnp.where(aux_ref[2:3, :] > 0, f, NEG)
    to_sublanes(f_ref, col_ref, f_ref.shape[1])
    col_lse(score_ref, col_ref, out_ref)


def row_kernel(score_ref, lse_ref, aux_ref, out_ref, g_ref, peak_ref, total_ref):
    g_ref[...] = aux_ref[1:2, :] - lse_ref[...] * aux_ref[0:1, :]
    row_lse(score_ref, g_ref, peak_ref, total_ref, out_ref)


def last_kernel(*refs, pieces, groups):
    slabs, refs = refs[: len(pieces)], refs[len(pieces) :]
    mine, refs = refs[:groups], refs[groups:]
    theirs, refs = refs[:groups], refs[groups:]
    f_all_ref, lse_ref, aux_ref, f_ref, _, out_ref, f_out, g_out, row_ref, col_ref, right_pad, sum_ref, turn_ref = refs
    share = slabs[0].shape[0]
    _, half, rows = mine[0].shape
    f_out[...] = f_ref[...] * (1.0 / SCALE)
    g_out[...] = (aux_ref[1:2, :] - lse_ref[...] * aux_ref[0:1, :]) * (1.0 / SCALE)
    own = pl.ds(pl.multiple_of(lax.axis_index("src") * share, share), share)
    row_ref[0:1, :] = jnp.where(aux_ref[0:1, own] > 0, -lse_ref[0:1, own], NEG)
    to_sublanes(row_ref, col_ref, share)
    spot = 0
    for slab_ref, (group, first) in zip(slabs, pieces):
        for b in range(slab_ref.shape[1] // rows):
            right_pad[0:half, :] = mine[group][first + b]
            right_pad[half:, :] = theirs[group][first + b]
            terms = jnp.concatenate(split(right_pad[...]), axis=0)
            add = wide(col_ref[...], rows) + f_all_ref[0:1, spot : spot + rows]
            high, mid, _ = split(jnp.exp2(slab_ref[:, b * rows : (b + 1) * rows] + add))
            sums = lax.dot_general(
                jnp.concatenate([high, mid], axis=1), jnp.concatenate([terms, terms], axis=1),
                (((1,), (1,)), ((), ())), preferred_element_type=jnp.float32,
            )
            if spot == 0:
                sum_ref[...] = sums
            else:
                sum_ref[...] += sums
            spot += rows
    sums = sum_ref[...].T
    turn_ref[...] = sums[0:DEPTH] + sums[DEPTH : 2 * DEPTH] + sums[2 * DEPTH :]
    core = lax.axis_index("tgt") % 2
    out_ref[0:half, :] = turn_ref[pl.ds(pl.multiple_of(core * half, half), half), :]
    out_ref[half:, :] = turn_ref[pl.ds(pl.multiple_of((1 - core) * half, half), half), :][: out_ref.shape[0] - half]


def merge(one, two):
    top = jnp.maximum(one, two)
    return top + jnp.log2(1.0 + jnp.exp2(jnp.minimum(one, two) - top))


def swap(value, axis, step):
    return lax.ppermute(value, axis, [(i, i ^ step) for i in range(lax.axis_size(axis))])


def doubling(size):
    return [1 << k for k in range(size.bit_length() - 1)]


def call(kernel, outs, scratch, ins, flops, expos=0, pin=True):
    return pl.pallas_call(
        kernel,
        out_shape=[(pltpu.VMEM if pin else jax.ShapeDtypeStruct)(shape, jnp.float32) for shape in outs],
        in_specs=[VMEM_SPEC] * len(ins),
        out_specs=[VMEM_SPEC] * len(outs),
        scratch_shapes=[pltpu.VMEM(*s) if isinstance(s[-1], type) else pltpu.VMEM(s, jnp.float32) for s in scratch],
        compiler_params=pltpu.CompilerParams(vmem_limit_bytes=VMEM_LIMIT),
        cost_estimate=pl.CostEstimate(flops=flops, bytes_accessed=0, transcendentals=expos),
    )(*[pinned(x) for x in ins])


def tie(*values):
    return lax.optimization_barrier(values)


class Beside:
    def __init__(self, half, token, own, steps):
        self.parts = half
        self.token = token
        self.own = own
        self.steps = list(steps)
        self.coming = None
        self.mine = []
        self.theirs = []
        self.todo = []
        self.done = []
        self.slabs = []

    def plain(self, value, axis, step):
        return swap(value, axis, step)

    def start(self, value, axis, step):
        if self.coming is not None or not self.steps:
            return swap(value, axis, step)
        value, self.parts = tie(value, self.parts)
        other = swap(value, axis, step)
        self.coming = swap(self.parts, "src", self.steps.pop(0))
        return other

    def land(self, value, delay=0):
        if self.coming is None:
            return value
        coming, self.coming = self.coming, None
        for _ in range(delay):
            self.token, coming = tie(self.token, coming)
            self.token = swap(self.token, "tgt", 1)
        value, coming, self.token = tie(value, coming, self.token)
        if self.steps:
            self.parts = jnp.concatenate([self.parts, coming], axis=0)
        else:
            self.mine = [self.parts, coming]
        return value

    def trade(self, value, axis, step):
        if len(self.theirs) == len(self.mine):
            return swap(value, axis, step)
        group = len(self.theirs)
        value, self.mine[group] = tie(value, self.mine[group])
        other = swap(value, axis, step)
        self.theirs.append(swap(self.mine[group], "tgt", 1))
        other, self.theirs[group] = tie(other, self.theirs[group])
        size = max(self.mine[group].shape[0] // 2, 1)
        self.todo += [(group, first, size) for first in range(0, self.mine[group].shape[0], size)]
        return other

    def piece(self):
        group, first, size = self.todo.pop(0)
        mine, theirs = self.mine[group], self.theirs[group]
        share = self.own.shape[1]
        rows = mine.shape[2]
        slab, token = call(
            functools.partial(slab_kernel, first=first),
            [(share, size * rows), (8, LANES)],
            [(DEPTH, rows), ((share, 6 * DEPTH), jnp.bfloat16), (8, share), (share, LANES)],
            [self.own, mine, theirs],
            12 * DEPTH * share * size * rows,
        )
        self.done.append((group, first))
        self.slabs.append(slab)
        return token

    def work(self, value, axis, step):
        if not self.todo:
            return swap(value, axis, step)
        value, self.own = tie(value, self.own)
        other = swap(value, axis, step)
        other, _ = tie(other, self.piece())
        return other

    def finish(self, value):
        while self.steps or self.coming is not None:
            if self.coming is None:
                self.coming = swap(self.parts, "src", self.steps.pop(0))
            value = self.land(value)
        while len(self.theirs) < len(self.mine):
            value = self.trade(value, "tgt", 1)
        while self.todo:
            self.piece()


def shards(sources, targets, pair_active, count_src, count_tgt):
    dims, rows = sources.shape
    cols = targets.shape[1]
    share = cols // lax.axis_size("src")
    column = (rows, LANES)
    pairs = rows * cols
    hbm = [pltpu.with_memory_space_constraint(x, pltpu.HBM) for x in (sources, targets, count_src, count_tgt)]
    outs = [(rows, cols), (1, rows), (8, rows), (8, cols), (DEPTH, share), (1, DEPTH // 2, rows), (1, LANES)]
    score, lse, row_aux, col_aux, own, half, token = pl.pallas_call(
        first_kernel,
        out_shape=[pltpu.VMEM(shape, jnp.float32) for shape in outs],
        in_specs=[pl.BlockSpec(memory_space=pltpu.HBM)] * 4 + [SMEM_SPEC],
        out_specs=[VMEM_SPEC] * len(outs),
        scratch_shapes=[
            pltpu.VMEM((dims, rows), jnp.float32),
            pltpu.VMEM((dims, cols), jnp.float32),
            pltpu.SMEM(count_src.shape, jnp.int32),
            pltpu.SMEM(count_tgt.shape, jnp.int32),
            pltpu.SemaphoreType.DMA((4,)),
            pltpu.VMEM((DEPTH, 512), jnp.float32),
            pltpu.VMEM((DEPTH, rows), jnp.float32),
            pltpu.VMEM((DEPTH, share), jnp.float32),
            pltpu.VMEM((rows, 6 * DEPTH), jnp.bfloat16),
            pltpu.VMEM((8, rows), jnp.float32),
            pltpu.VMEM(column, jnp.float32),
            pltpu.VMEM(column, jnp.float32),
            pltpu.VMEM(column, jnp.float32),
        ],
        compiler_params=pltpu.CompilerParams(vmem_limit_bytes=VMEM_LIMIT),
        cost_estimate=pl.CostEstimate(flops=12 * DEPTH * pairs, bytes_accessed=0, transcendentals=pairs),
    )(*hbm, pair_active)
    over_tgt = doubling(lax.axis_size("tgt"))
    over_src = doubling(lax.axis_size("src"))
    over_src = over_src[1:] + over_src[:1]
    side = Beside(half, token, own, over_src)
    beside = {
        (0, "tgt", over_tgt[-1]): side.start,
        (0, "src", over_src[-1]): side.start,
        (1, "src", over_src[-1]): side.start,
        (2, "src", over_src[0]): side.trade,
        (2, "src", over_src[1 % len(over_src)]): side.trade,
    }
    for step in range(ITERS):
        for bit in over_tgt:
            exchange = beside.get((step, "tgt", bit), side.work if step > 1 and bit == over_tgt[-1] else side.plain)
            lse = merge(lse, exchange(lse, "tgt", bit))
        if step > 1:
            lse = side.land(lse)
        lse, f, masked = call(
            col_kernel, [(1, cols), (1, rows), (1, rows)], [column], [score, lse, row_aux], 4 * pairs, pairs
        )
        if step < 2:
            lse = side.land(lse)
        if step < ITERS - 1:
            for bit in over_src:
                exchange = beside.get((step, "src", bit), side.work)
                lse = merge(lse, exchange(lse, "src", bit))
            lse, _ = call(
                row_kernel, [(1, rows), (1, cols)], [column, column], [score, lse, col_aux], 4 * pairs, pairs
            )
    for bit in over_src:
        both = jnp.concatenate([lse, masked], axis=1)
        other = side.work(both, "src", bit)
        lse = merge(lse, other[:, :cols])
        masked = jnp.concatenate([masked, other[:, cols:]], axis=1)
    side.finish(lse)
    ancestors, f, g = call(
        functools.partial(last_kernel, pieces=side.done, groups=len(side.mine)),
        [(dims, share), (1, rows), (1, cols)],
        [(8, share), (share, LANES), (DEPTH, rows), (share, 3 * DEPTH), (DEPTH, share)],
        [*side.slabs, *side.mine, *side.theirs, masked, lse, col_aux, f, side.token],
        18 * DEPTH * pairs, pairs, pin=False,
    )
    return (f[0], g[0], ancestors)


def solution(mesh):
    return jax.shard_map(
        shards,
        mesh=mesh,
        in_specs=(P(None, "src"), P(None, "tgt"), P("src", "tgt"), P(), P()),
        out_specs=(P("src"), P("tgt"), P(None, ("tgt", "src"))),
        check_vma=False,
    )
```

time: 523 us -> 116 us (0.22)
  blocking collectives: 319 us -> 0 us
  other arithmetic: 85.2 us -> 0.97 us
  Pallas kernels: 0 us -> 42.2 us
  waiting for transfers between devices: 73.7 us -> 37.9 us
  starting transfers between devices: 0.04 us -> 33.2 us
  matrix products: 23.9 us -> 0 us
  between operations: 16.2 us -> 1.44 us
    pmax x8 -> x0, blocking collectives: 162 us -> none  [the longest x4 136 us: shards(): best = lax.pmax(peak, 'src')]
    psum x8 -> x0, blocking collectives: 157 us -> none  [the longest x4 132 us: shards(): total = lax.psum(total * jnp.exp(peak - best), 'src')]
    psum x1 -> x0, waiting for transfers between devices: 73.7 us -> none  [shards(): summed = lax.psum(whole, 'src')]
    reduce_sum x12 -> x0, other arithmetic: 47.3 us -> none  [the longest x4 21.4 us: shards(): jnp.sum(jnp.where(allowed, jnp.exp(logits - peak[:, None]), 0.0), axis=1)]
    pallas_call x0 -> x13, Pallas kernels: none -> 42.2 us  [the longest x12 34.3 us: call(): pl.pallas_call(kernel, out_shape=[(pltpu.VMEM if pin else jax.ShapeDtypeS...]
    ppermute x0 -> x25, waiting for transfers between devices: none -> 37.9 us  [swap(): lax.ppermute(value, axis, [(i, i ^ step) for i in range(lax.axis_size(axi...]
    ppermute x0 -> x25, starting transfers between devices: none -> 33.2 us  [swap(): lax.ppermute(value, axis, [(i, i ^ step) for i in range(lax.axis_size(axi...]
    reduce_max x7 -> x0, other arithmetic: 31.3 us -> none  [the longest x4 17.8 us: shards(): peak = jnp.max(logits, axis=0)]
  transfers between devices with their start and end apart: 1 -> 25, of which waited for: 1 -> 19; matrix products, arithmetic and copies ran while one was open for 0% -> 0% of each run, Pallas kernels for 0% -> 11%
where the time goes in v1:
time: 116 us
  Pallas kernels  42.2 us (36%)
  waiting for transfers between devices  37.9 us (33%)
  starting transfers between devices  33.2 us (29%)
  between operations  1.44 us (1%)
    ppermute x25, waiting for transfers between devices, swap(): lax.ppermute(value, axis, [(i, i ^ step) for i in range(lax.axis_size(axi...  37.9 us
    pallas_call x12, Pallas kernels, call(): pl.pallas_call(kernel, out_shape=[(pltpu.VMEM if pin else jax.ShapeDtypeS...  34.3 us
    ppermute x25, starting transfers between devices, swap(): lax.ppermute(value, axis, [(i, i ^ step) for i in range(lax.axis_size(axi...  33.2 us
    pallas_call x1, Pallas kernels, shards(): pl.pallas_call(first_kernel, out_shape=[pltpu.VMEM(shape, jnp.float32) fo...  7.93 us
  transfers between devices with their start and end apart: 25, of which 19 were waited for; matrix products, arithmetic and copies ran while one was open for 0% of the time, Pallas kernels for 11%

profile of v1, /device:TPU:0, one launch (start us, length us, event | category | flops | bytes accessed | tf_op | source)
XLA Modules:
  0.0 115.8 jit_solution(4221115428216126821)
XLA Ops:
  1.3 7.9 %shard_map.76 = (f32[512,4096]{1,0:T(8,128)S(1)}, f32[1,512]{1,0:T(1,128)S(1)}, f32[8,512]{1,0:T(8,128)S(1)}, f32[8,4096]{1,0:T(8,128)S(1)}, f32[64,512]{1,0:T(8...) custom-call(f32[50,512]{1,0:T(8,128)} %src_hbm.1, f32[50,4096]{1,0:T(8,128)} %tgt_hbm.1, s32[8]{0:T(128)} %count_src_hbm.1, ...), custom_call_target="tpu_custom_call" | custom-call | flops 1610612736 | tf_op jit(solution)/shard_map/pallas_call | solution.py:368
  10.6 2.9 %collective-permute-start.1 = (f32[1,512]{1,0:T(1,128)S(1)}, f32[1,512]{1,0:T(1,128)S(1)}, u32[]{:S(2)}, u32[]{:S(2)}) collective-permute-start(f32[1,512]{1,0:T(1,128)S(1)} %multiply_add_fusion.19), channel_id=1, source_target_pairs={{0,2},{1,3},{2,0},{3,1},{4,6},{5,7},{6,4},{7,5},{8,10},{9,11},{10,... | collective-permute-start | bytes 6152 | tf_op jit(solution)/shard_map/ppermute | solution.py:252
  13.5 1.6 %collective-permute-start.2 = (f32[1,32,512]{2,1,0:T(8,128)S(1)}, f32[1,32,512]{2,1,0:T(8,128)S(1)}, u32[]{:S(2)}, u32[]{:S(2)}) collective-permute-start(f32[1,32,512]{2,1,0:T(8,128)S(1)} %get-tuple-element.63), channel_id=1, source_target_pairs={{0,8},{4,12},{8,0},{12,4},{16,24},{20,28},{24,16},{28,20},{1,9},{5... | collective-permute-start | bytes 196616 | tf_op jit(solution)/shard_map/ppermute | solution.py:252
  15.1 3.6 %shard_map.77 = (f32[1,4096]{1,0:T(1,128)S(1)}, f32[1,512]{1,0:T(1,128)}, f32[1,512]{1,0:T(1,128)}) custom-call(f32[512,4096]{1,0:T(8,128)S(1)} %get-tuple-element.57.score_ref, f32[1,512]{1,0:T(1,128)S(1)} %multiply_add_fusion.18.lse_ref, f32[8,512]{1,0:T(8,128)S(1)} %get-tuple-element.61.aux_ref), custom_call_target="tpu_custom_call" | custom-call | flops 8388608 | tf_op jit(solution)/shard_map/pallas_call | solution.py:260
  18.7 2.1 %collective-permute-start.3 = (f32[1,4096]{1,0:T(1,128)S(1)}, f32[1,4096]{1,0:T(1,128)S(1)}, u32[]{:S(2)}, u32[]{:S(2)}) collective-permute-start(f32[1,4096]{1,0:T(1,128)S(1)} %get-tuple-element.65), channel_id=1, source_target_pairs={{0,8},{4,12},{8,0},{12,4},{16,24},{20,28},{24,16},{28,20},{1,9},{5... | collective-permute-start | bytes 49160 | tf_op jit(solution)/shard_map/ppermute | solution.py:252
  20.8 1.7 %collective-permute-done.3 = f32[1,4096]{1,0:T(1,128)S(1)} collective-permute-done((f32[1,4096]{1,0:T(1,128)S(1)}, f32[1,4096]{1,0:T(1,128)S(1)}, u32[]{:S(2)}, u32[]{:S(2)}) %collective-permute-start.3) | collective-permute-done | bytes 16416 | tf_op jit(solution)/shard_map/ppermute | solution.py:252
  22.6 3.1 %collective-permute-start.4 = (f32[1,4096]{1,0:T(1,128)S(1)}, f32[1,4096]{1,0:T(1,128)S(1)}, u32[]{:S(2)}, u32[]{:S(2)}) collective-permute-start(f32[1,4096]{1,0:T(1,128)S(1)} %multiply_add_fusion.11), channel_id=1, source_target_pairs={{0,16},{4,20},{8,24},{12,28},{16,0},{20,4},{24,8},{28,12},{1,17},{... | collective-permute-start | bytes 49160 | tf_op jit(solution)/shard_map/ppermute | solution.py:252
  25.7 1.7 %collective-permute-done.4 = f32[1,4096]{1,0:T(1,128)S(1)} collective-permute-done((f32[1,4096]{1,0:T(1,128)S(1)}, f32[1,4096]{1,0:T(1,128)S(1)}, u32[]{:S(2)}, u32[]{:S(2)}) %collective-permute-start.4) | collective-permute-done | bytes 16416 | tf_op jit(solution)/shard_map/ppermute | solution.py:252
  27.4 1.9 %collective-permute-start.5 = (f32[1,4096]{1,0:T(1,128)S(1)}, f32[1,4096]{1,0:T(1,128)S(1)}, u32[]{:S(2)}, u32[]{:S(2)}) collective-permute-start(f32[1,4096]{1,0:T(1,128)S(1)} %multiply_add_fusion.10), channel_id=1, source_target_pairs={{0,4},{4,0},{8,12},{12,8},{16,20},{20,16},{24,28},{28,24},{1,5},{5... | collective-permute-start | bytes 49160 | tf_op jit(solution)/shard_map/ppermute | solution.py:252
  29.3 1.9 %collective-permute-done.5 = f32[1,4096]{1,0:T(1,128)S(1)} collective-permute-done((f32[1,4096]{1,0:T(1,128)S(1)}, f32[1,4096]{1,0:T(1,128)S(1)}, u32[]{:S(2)}, u32[]{:S(2)}) %collective-permute-start.5) | collective-permute-done | bytes 16416 | tf_op jit(solution)/shard_map/ppermute | solution.py:252
  31.3 3.5 %shard_map.78 = (f32[1,512]{1,0:T(1,128)S(1)}, f32[1,4096]{1,0:T(1,128)}) custom-call(f32[512,4096]{1,0:T(8,128)S(1)} %get-tuple-element.57.score_ref, f32[1,4096]{1,0:T(1,128)S(1)} %multiply_add_fusion.9.lse_ref, f32[8,4096]{1,0:T(8,128)S(1)} %get-tuple-element.68.aux_ref.refs_10_), custom_call_target="tpu_custom_call" | custom-call | flops 8388608 | tf_op jit(solution)/shard_map/pallas_call | solution.py:260
  36.0 1.9 %collective-permute-start.7 = (f32[1,512]{1,0:T(1,128)S(1)}, f32[1,512]{1,0:T(1,128)S(1)}, u32[]{:S(2)}, u32[]{:S(2)}) collective-permute-start(f32[1,512]{1,0:T(1,128)S(1)} %multiply_add_fusion.17), channel_id=1, source_target_pairs={{0,2},{1,3},{2,0},{3,1},{4,6},{5,7},{6,4},{7,5},{8,10},{9,11},{10,... | collective-permute-start | bytes 6152 | tf_op jit(solution)/shard_map/ppermute | solution.py:252
  37.9 2.6 %collective-permute-start.8 = (f32[2,32,512]{2,1,0:T(8,128)S(1)}, f32[2,32,512]{2,1,0:T(8,128)S(1)}, u32[]{:S(2)}, u32[]{:S(2)}) collective-permute-start(f32[2,32,512]{2,1,0:T(8,128)S(1)} %pad_maximum_fusion.1), channel_id=1, source_target_pairs={{0,16},{4,20},{8,24},{12,28},{16,0},{20,4},{24,8},{28,12},{1,17},{... | collective-permute-start | bytes 393224 | tf_op jit(solution)/shard_map/ppermute | solution.py:252
  40.5 3.6 %shard_map.79 = (f32[1,4096]{1,0:T(1,128)S(1)}, f32[1,512]{1,0:T(1,128)}, f32[1,512]{1,0:T(1,128)}) custom-call(f32[512,4096]{1,0:T(8,128)S(1)} %get-tuple-element.57.score_ref, f32[1,512]{1,0:T(1,128)S(1)} %multiply_add_fusion.16.lse_ref, f32[8,512]{1,0:T(8,128)S(1)} %get-tuple-element.61.aux_ref), custom_call_target="tpu_custom_call" | custom-call | flops 8388608 | tf_op jit(solution)/shard_map/pallas_call | solution.py:260
  44.2 2.8 %collective-permute-done.8 = f32[2,32,512]{2,1,0:T(8,128)S(1)} collective-permute-done((f32[2,32,512]{2,1,0:T(8,128)S(1)}, f32[2,32,512]{2,1,0:T(8,128)S(1)}, u32[]{:S(2)}, u32[]{:S(2)}) %collective-permute-start.8) | collective-permute-done | bytes 131104 | tf_op jit(solution)/shard_map/ppermute | solution.py:252
  47.6 3.1 %collective-permute-done.9 = f32[1,4096]{1,0:T(1,128)S(1)} collective-permute-done((f32[1,4096]{1,0:T(1,128)S(1)}, f32[1,4096]{1,0:T(1,128)S(1)}, u32[]{:S(2)}, u32[]{:S(2)}) %collective-permute-start.9) | collective-permute-done | bytes 16416 | tf_op jit(solution)/shard_map/ppermute | solution.py:252
  50.7 2.1 %collective-permute-start.10 = (f32[1,4096]{1,0:T(1,128)S(1)}, f32[1,4096]{1,0:T(1,128)S(1)}, u32[]{:S(2)}, u32[]{:S(2)}) collective-permute-start(f32[1,4096]{1,0:T(1,128)S(1)} %multiply_add_fusion.8), channel_id=1, source_target_pairs={{0,16},{4,20},{8,24},{12,28},{16,0},{20,4},{24,8},{28,12},{1,17},{... | collective-permute-start | bytes 49160 | tf_op jit(solution)/shard_map/ppermute | solution.py:252
  52.9 2.6 %collective-permute-done.10 = f32[1,4096]{1,0:T(1,128)S(1)} collective-permute-done((f32[1,4096]{1,0:T(1,128)S(1)}, f32[1,4096]{1,0:T(1,128)S(1)}, u32[]{:S(2)}, u32[]{:S(2)}) %collective-permute-start.10) | collective-permute-done | bytes 16416 | tf_op jit(solution)/shard_map/ppermute | solution.py:252
  57.1 2.2 %collective-permute-done.11 = f32[1,4096]{1,0:T(1,128)S(1)} collective-permute-done((f32[1,4096]{1,0:T(1,128)S(1)}, f32[1,4096]{1,0:T(1,128)S(1)}, u32[]{:S(2)}, u32[]{:S(2)}) %collective-permute-start.11) | collective-permute-done | bytes 16416 | tf_op jit(solution)/shard_map/ppermute | solution.py:252
  59.4 3.5 %shard_map.80 = (f32[1,512]{1,0:T(1,128)S(1)}, f32[1,4096]{1,0:T(1,128)}) custom-call(f32[512,4096]{1,0:T(8,128)S(1)} %get-tuple-element.57.score_ref, f32[1,4096]{1,0:T(1,128)S(1)} %multiply_add_fusion.6.lse_ref, f32[8,4096]{1,0:T(8,128)S(1)} %get-tuple-element.68.aux_ref.refs_10_), custom_call_target="tpu_custom_call" | custom-call | flops 8388608 | tf_op jit(solution)/shard_map/pallas_call | solution.py:260
  65.0 3.1 %collective-permute-done.13 = f32[1,512]{1,0:T(1,128)S(1)} collective-permute-done((f32[1,512]{1,0:T(1,128)S(1)}, f32[1,512]{1,0:T(1,128)S(1)}, u32[]{:S(2)}, u32[]{:S(2)}) %collective-permute-start.13) | collective-permute-done | bytes 2080 | tf_op jit(solution)/shard_map/ppermute | solution.py:252
  68.1 3.5 %collective-permute-done.14.mine_ref.refs_5_ = f32[4,32,512]{2,1,0:T(8,128)S(1)} collective-permute-done((f32[4,32,512]{2,1,0:T(8,128)S(1)}, f32[4,32,512]{2,1,0:T(8,128)S(1)}, u32[]{:S(2)}, u32[]{:S(2)}) %collective-permute-start.14) | collective-permute-done | bytes 262176 | tf_op jit(solution)/shard_map/ppermute | solution.py:252
  71.6 3.6 %shard_map.81 = (f32[1,4096]{1,0:T(1,128)S(1)}, f32[1,512]{1,0:T(1,128)}, f32[1,512]{1,0:T(1,128)}) custom-call(f32[512,4096]{1,0:T(8,128)S(1)} %get-tuple-element.57.score_ref, f32[1,512]{1,0:T(1,128)S(1)} %multiply_add_fusion.14.lse_ref, f32[8,512]{1,0:T(8,128)S(1)} %get-tuple-element.61.aux_ref), custom_call_target="tpu_custom_call" | custom-call | flops 8388608 | tf_op jit(solution)/shard_map/pallas_call | solution.py:260
  76.4 2.6 %collective-permute-done.15 = f32[1,4096]{1,0:T(1,128)S(1)} collective-permute-done((f32[1,4096]{1,0:T(1,128)S(1)}, f32[1,4096]{1,0:T(1,128)S(1)}, u32[]{:S(2)}, u32[]{:S(2)}) %collective-permute-start.15) | collective-permute-done | bytes 16416 | tf_op jit(solution)/shard_map/ppermute | solution.py:252
  79.1 2.1 %collective-permute-start.17 = (f32[1,4096]{1,0:T(1,128)S(1)}, f32[1,4096]{1,0:T(1,128)S(1)}, u32[]{:S(2)}, u32[]{:S(2)}) collective-permute-start(f32[1,4096]{1,0:T(1,128)S(1)} %multiply_add_fusion.5), channel_id=1, source_target_pairs={{0,16},{4,20},{8,24},{12,28},{16,0},{20,4},{24,8},{28,12},{1,17},{... | collective-permute-start | bytes 49160 | tf_op jit(solution)/shard_map/ppermute | solution.py:252
  81.2 2.6 %collective-permute-done.17 = f32[1,4096]{1,0:T(1,128)S(1)} collective-permute-done((f32[1,4096]{1,0:T(1,128)S(1)}, f32[1,4096]{1,0:T(1,128)S(1)}, u32[]{:S(2)}, u32[]{:S(2)}) %collective-permute-start.17) | collective-permute-done | bytes 16416 | tf_op jit(solution)/shard_map/ppermute | solution.py:252
  85.5 2.2 %collective-permute-done.19 = f32[1,4096]{1,0:T(1,128)S(1)} collective-permute-done((f32[1,4096]{1,0:T(1,128)S(1)}, f32[1,4096]{1,0:T(1,128)S(1)}, u32[]{:S(2)}, u32[]{:S(2)}) %collective-permute-start.19) | collective-permute-done | bytes 16416 | tf_op jit(solution)/shard_map/ppermute | solution.py:252
  87.8 3.5 %shard_map.83 = (f32[1,512]{1,0:T(1,128)S(1)}, f32[1,4096]{1,0:T(1,128)}) custom-call(f32[512,4096]{1,0:T(8,128)S(1)} %get-tuple-element.57.score_ref, f32[1,4096]{1,0:T(1,128)S(1)} %multiply_add_fusion.3.lse_ref, f32[8,4096]{1,0:T(8,128)S(1)} %get-tuple-element.68.aux_ref.refs_10_), custom_call_target="tpu_custom_call" | custom-call | flops 8388608 | tf_op jit(solution)/shard_map/pallas_call | solution.py:260
  94.5 1.6 %collective-permute-done.21 = f32[1,512]{1,0:T(1,128)S(1)} collective-permute-done((f32[1,512]{1,0:T(1,128)S(1)}, f32[1,512]{1,0:T(1,128)S(1)}, u32[]{:S(2)}, u32[]{:S(2)}) %collective-permute-start.21) | collective-permute-done | bytes 2080 | tf_op jit(solution)/shard_map/ppermute | solution.py:252
  96.2 3.1 %shard_map.85 = (f32[1,4096]{1,0:T(1,128)S(1)}, f32[1,512]{1,0:T(1,128)S(1)}, f32[1,512]{1,0:T(1,128)S(1)}) custom-call(f32[512,4096]{1,0:T(8,128)S(1)} %get-tuple-element.57.score_ref, f32[1,512]{1,0:T(1,128)S(1)} %multiply_add_fusion.12.lse_ref, f32[8,512]{1,0:T(8,128)S(1)} %get-tuple-element.61.aux_ref), custom_call_target="tpu_custom_call" | custom-call | flops 8388608 | tf_op jit(solution)/shard_map/pallas_call | solution.py:260
  103.2 2.1 %collective-permute-start.23 = (f32[1,5120]{1,0:T(1,128)S(1)}, f32[1,5120]{1,0:T(1,128)S(1)}, u32[]{:S(2)}, u32[]{:S(2)}) collective-permute-start(f32[1,5120]{1,0:T(1,128)S(1)} %pad_maximum_fusion.3), channel_id=1, source_target_pairs={{0,16},{4,20},{8,24},{12,28},{16,0},{20,4},{24,8},{28,12},{1,17},{... | collective-permute-start | bytes 61448 | tf_op jit(solution)/shard_map/ppermute | solution.py:252
  112.1 3.7 %shard_map.88 = (f32[50,512]{1,0:T(8,128)}, f32[1,512]{1,0:T(1,128)}, f32[1,4096]{1,0:T(1,128)}) custom-call(f32[512,1024]{1,0:T(8,128)S(1)} %get-tuple-element.91.refs_0_, f32[512,1024]{1,0:T(8,128)S(1)} %get-tuple-element.95.refs_1_, f32[512,1024]{1,0:T(8,128)S(1)} %get-tuple-element.101.refs_2_, f32[512,1024]{1,0:T(8,128)S(1)} %get-tuple-element.104.refs_3_, ...), custom_call_target="tpu_custom_call" | custom-call | flops 2415919104 | tf_op jit(solution)/shard_map/pallas_call | solution.py:260
  (59 shorter events, 24.1 us)
Async XLA Ops:
  9.2 1.3 %collective-permute-start = (f32[1,512]{1,0:T(1,128)S(1)}, f32[1,512]{1,0:T(1,128)S(1)}, u32[]{:S(2)}, u32[]{:S(2)}) collective-permute-start(f32[1,512]{1,0:T(1,128)S(1)} %get-tuple-element.58), channel_id=1, source_target_pairs={{0,1},{1,0},{2,3},{3,2},{4,5},{5,4},{6,7},{7,6},{8,9},{9,8},{10,11... | collective-permute-start | bytes 6152 | tf_op jit(solution)/shard_map/ppermute | solution.py:252
  10.6 4.5 %collective-permute-start.1 = (f32[1,512]{1,0:T(1,128)S(1)}, f32[1,512]{1,0:T(1,128)S(1)}, u32[]{:S(2)}, u32[]{:S(2)}) collective-permute-start(f32[1,512]{1,0:T(1,128)S(1)} %multiply_add_fusion.19), channel_id=1, source_target_pairs={{0,2},{1,3},{2,0},{3,1},{4,6},{5,7},{6,4},{7,5},{8,10},{9,11},{10,... | collective-permute-start | bytes 6152 | tf_op jit(solution)/shard_map/ppermute | solution.py:252
  13.5 5.2 %collective-permute-start.2 = (f32[1,32,512]{2,1,0:T(8,128)S(1)}, f32[1,32,512]{2,1,0:T(8,128)S(1)}, u32[]{:S(2)}, u32[]{:S(2)}) collective-permute-start(f32[1,32,512]{2,1,0:T(8,128)S(1)} %get-tuple-element.63), channel_id=1, source_target_pairs={{0,8},{4,12},{8,0},{12,4},{16,24},{20,28},{24,16},{28,20},{1,9},{5... | collective-permute-start | bytes 196616 | tf_op jit(solution)/shard_map/ppermute | solution.py:252
  18.7 3.8 %collective-permute-start.3 = (f32[1,4096]{1,0:T(1,128)S(1)}, f32[1,4096]{1,0:T(1,128)S(1)}, u32[]{:S(2)}, u32[]{:S(2)}) collective-permute-start(f32[1,4096]{1,0:T(1,128)S(1)} %get-tuple-element.65), channel_id=1, source_target_pairs={{0,8},{4,12},{8,0},{12,4},{16,24},{20,28},{24,16},{28,20},{1,9},{5... | collective-permute-start | bytes 49160 | tf_op jit(solution)/shard_map/ppermute | solution.py:252
  22.6 4.8 %collective-permute-start.4 = (f32[1,4096]{1,0:T(1,128)S(1)}, f32[1,4096]{1,0:T(1,128)S(1)}, u32[]{:S(2)}, u32[]{:S(2)}) collective-permute-start(f32[1,4096]{1,0:T(1,128)S(1)} %multiply_add_fusion.11), channel_id=1, source_target_pairs={{0,16},{4,20},{8,24},{12,28},{16,0},{20,4},{24,8},{28,12},{1,17},{... | collective-permute-start | bytes 49160 | tf_op jit(solution)/shard_map/ppermute | solution.py:252
  27.4 3.8 %collective-permute-start.5 = (f32[1,4096]{1,0:T(1,128)S(1)}, f32[1,4096]{1,0:T(1,128)S(1)}, u32[]{:S(2)}, u32[]{:S(2)}) collective-permute-start(f32[1,4096]{1,0:T(1,128)S(1)} %multiply_add_fusion.10), channel_id=1, source_target_pairs={{0,4},{4,0},{8,12},{12,8},{16,20},{20,16},{24,28},{28,24},{1,5},{5... | collective-permute-start | bytes 49160 | tf_op jit(solution)/shard_map/ppermute | solution.py:252
  34.8 1.2 collective-permute-start.6
  36.0 4.5 %collective-permute-start.7 = (f32[1,512]{1,0:T(1,128)S(1)}, f32[1,512]{1,0:T(1,128)S(1)}, u32[]{:S(2)}, u32[]{:S(2)}) collective-permute-start(f32[1,512]{1,0:T(1,128)S(1)} %multiply_add_fusion.17), channel_id=1, source_target_pairs={{0,2},{1,3},{2,0},{3,1},{4,6},{5,7},{6,4},{7,5},{8,10},{9,11},{10,... | collective-permute-start | bytes 6152 | tf_op jit(solution)/shard_map/ppermute | solution.py:252
  37.9 9.0 %collective-permute-start.8 = (f32[2,32,512]{2,1,0:T(8,128)S(1)}, f32[2,32,512]{2,1,0:T(8,128)S(1)}, u32[]{:S(2)}, u32[]{:S(2)}) collective-permute-start(f32[2,32,512]{2,1,0:T(8,128)S(1)} %pad_maximum_fusion.1), channel_id=1, source_target_pairs={{0,16},{4,20},{8,24},{12,28},{16,0},{20,4},{24,8},{28,12},{1,17},{... | collective-permute-start | bytes 393224 | tf_op jit(solution)/shard_map/ppermute | solution.py:252
  46.9 3.7 %collective-permute-start.9 = (f32[1,4096]{1,0:T(1,128)S(1)}, f32[1,4096]{1,0:T(1,128)S(1)}, u32[]{:S(2)}, u32[]{:S(2)}) collective-permute-start(f32[1,4096]{1,0:T(1,128)S(1)} %get-tuple-element.73), channel_id=1, source_target_pairs={{0,8},{4,12},{8,0},{12,4},{16,24},{20,28},{24,16},{28,20},{1,9},{5... | collective-permute-start | bytes 49160 | tf_op jit(solution)/shard_map/ppermute | solution.py:252
  50.7 4.7 %collective-permute-start.10 = (f32[1,4096]{1,0:T(1,128)S(1)}, f32[1,4096]{1,0:T(1,128)S(1)}, u32[]{:S(2)}, u32[]{:S(2)}) collective-permute-start(f32[1,4096]{1,0:T(1,128)S(1)} %multiply_add_fusion.8), channel_id=1, source_target_pairs={{0,16},{4,20},{8,24},{12,28},{16,0},{20,4},{24,8},{28,12},{1,17},{... | collective-permute-start | bytes 49160 | tf_op jit(solution)/shard_map/ppermute | solution.py:252
  55.5 3.8 %collective-permute-start.11 = (f32[1,4096]{1,0:T(1,128)S(1)}, f32[1,4096]{1,0:T(1,128)S(1)}, u32[]{:S(2)}, u32[]{:S(2)}) collective-permute-start(f32[1,4096]{1,0:T(1,128)S(1)} %multiply_add_fusion.7), channel_id=1, source_target_pairs={{0,4},{4,0},{8,12},{12,8},{16,20},{20,16},{24,28},{28,24},{1,5},{5... | collective-permute-start | bytes 49160 | tf_op jit(solution)/shard_map/ppermute | solution.py:252
  62.9 1.5 %collective-permute-start.12 = (f32[1,512]{1,0:T(1,128)S(1)}, f32[1,512]{1,0:T(1,128)S(1)}, u32[]{:S(2)}, u32[]{:S(2)}) collective-permute-start(f32[1,512]{1,0:T(1,128)S(1)} %get-tuple-element.76), channel_id=1, source_target_pairs={{0,1},{1,0},{2,3},{3,2},{4,5},{5,4},{6,7},{7,6},{8,9},{9,8},{10,11... | collective-permute-start | bytes 6152 | tf_op jit(solution)/shard_map/ppermute | solution.py:252
  62.9 8.7 %collective-permute-start.14 = (f32[4,32,512]{2,1,0:T(8,128)S(1)}, f32[4,32,512]{2,1,0:T(8,128)S(1)}, u32[]{:S(2)}, u32[]{:S(2)}) collective-permute-start(f32[4,32,512]{2,1,0:T(8,128)S(1)} %pad_maximum_fusion.mine_ref.refs_4_), channel_id=1, source_target_pairs={{0,4},{4,0},{8,12},{12,8},{16,20},{20,16},{24,28},{28,24},{1,5},{5... | collective-permute-start | bytes 786440 | tf_op jit(solution)/shard_map/ppermute | solution.py:252
  64.4 3.7 %collective-permute-start.13 = (f32[1,512]{1,0:T(1,128)S(1)}, f32[1,512]{1,0:T(1,128)S(1)}, u32[]{:S(2)}, u32[]{:S(2)}) collective-permute-start(f32[1,512]{1,0:T(1,128)S(1)} %multiply_add_fusion.15), channel_id=1, source_target_pairs={{0,2},{1,3},{2,0},{3,1},{4,6},{5,7},{6,4},{7,5},{8,10},{9,11},{10,... | collective-permute-start | bytes 6152 | tf_op jit(solution)/shard_map/ppermute | solution.py:252
  75.2 3.7 %collective-permute-start.16 = (f32[4,32,512]{2,1,0:T(8,128)S(1)}, f32[4,32,512]{2,1,0:T(8,128)S(1)}, u32[]{:S(2)}, u32[]{:S(2)}) collective-permute-start(f32[4,32,512]{2,1,0:T(8,128)S(1)} %pad_maximum_fusion.mine_ref.refs_4_), channel_id=1, source_target_pairs={{0,1},{1,0},{2,3},{3,2},{4,5},{5,4},{6,7},{7,6},{8,9},{9,8},{10,11... | collective-permute-start | bytes 786440 | tf_op jit(solution)/shard_map/ppermute | solution.py:252
  75.2 3.7 %collective-permute-start.15 = (f32[1,4096]{1,0:T(1,128)S(1)}, f32[1,4096]{1,0:T(1,128)S(1)}, u32[]{:S(2)}, u32[]{:S(2)}) collective-permute-start(f32[1,4096]{1,0:T(1,128)S(1)} %get-tuple-element.81), channel_id=1, source_target_pairs={{0,8},{4,12},{8,0},{12,4},{16,24},{20,28},{24,16},{28,20},{1,9},{5... | collective-permute-start | bytes 49160 | tf_op jit(solution)/shard_map/ppermute | solution.py:252
  79.1 4.8 %collective-permute-start.18 = (f32[4,32,512]{2,1,0:T(8,128)S(1)}, f32[4,32,512]{2,1,0:T(8,128)S(1)}, u32[]{:S(2)}, u32[]{:S(2)}) collective-permute-start(f32[4,32,512]{2,1,0:T(8,128)S(1)} %collective-permute-done.14.mine_ref.refs_5_), channel_id=1, source_target_pairs={{0,1},{1,0},{2,3},{3,2},{4,5},{5,4},{6,7},{7,6},{8,9},{9,8},{10,11... | collective-permute-start | bytes 786440 | tf_op jit(solution)/shard_map/ppermute | solution.py:252
  79.1 4.7 %collective-permute-start.17 = (f32[1,4096]{1,0:T(1,128)S(1)}, f32[1,4096]{1,0:T(1,128)S(1)}, u32[]{:S(2)}, u32[]{:S(2)}) collective-permute-start(f32[1,4096]{1,0:T(1,128)S(1)} %multiply_add_fusion.5), channel_id=1, source_target_pairs={{0,16},{4,20},{8,24},{12,28},{16,0},{20,4},{24,8},{28,12},{1,17},{... | collective-permute-start | bytes 49160 | tf_op jit(solution)/shard_map/ppermute | solution.py:252
  83.9 3.8 %collective-permute-start.19 = (f32[1,4096]{1,0:T(1,128)S(1)}, f32[1,4096]{1,0:T(1,128)S(1)}, u32[]{:S(2)}, u32[]{:S(2)}) collective-permute-start(f32[1,4096]{1,0:T(1,128)S(1)} %multiply_add_fusion.4), channel_id=1, source_target_pairs={{0,4},{4,0},{8,12},{12,8},{16,20},{20,16},{24,28},{28,24},{1,5},{5... | collective-permute-start | bytes 49160 | tf_op jit(solution)/shard_map/ppermute | solution.py:252
  91.3 1.2 collective-permute-start.20
  92.5 3.7 %collective-permute-start.21 = (f32[1,512]{1,0:T(1,128)S(1)}, f32[1,512]{1,0:T(1,128)S(1)}, u32[]{:S(2)}, u32[]{:S(2)}) collective-permute-start(f32[1,512]{1,0:T(1,128)S(1)} %multiply_add_fusion.13), channel_id=1, source_target_pairs={{0,2},{1,3},{2,0},{3,1},{4,6},{5,7},{6,4},{7,5},{8,10},{9,11},{10,... | collective-permute-start | bytes 6152 | tf_op jit(solution)/shard_map/ppermute | solution.py:252
  99.3 3.8 %collective-permute-start.22 = (f32[1,4608]{1,0:T(1,128)S(1)}, f32[1,4608]{1,0:T(1,128)S(1)}, u32[]{:S(2)}, u32[]{:S(2)}) collective-permute-start(f32[1,4608]{1,0:T(1,128)S(1)} %pad_maximum_fusion.4), channel_id=1, source_target_pairs={{0,8},{4,12},{8,0},{12,4},{16,24},{20,28},{24,16},{28,20},{1,9},{5... | collective-permute-start | bytes 55304 | tf_op jit(solution)/shard_map/ppermute | solution.py:252
  103.2 4.7 %collective-permute-start.23 = (f32[1,5120]{1,0:T(1,128)S(1)}, f32[1,5120]{1,0:T(1,128)S(1)}, u32[]{:S(2)}, u32[]{:S(2)}) collective-permute-start(f32[1,5120]{1,0:T(1,128)S(1)} %pad_maximum_fusion.3), channel_id=1, source_target_pairs={{0,16},{4,20},{8,24},{12,28},{16,0},{20,4},{24,8},{28,12},{1,17},{... | collective-permute-start | bytes 61448 | tf_op jit(solution)/shard_map/ppermute | solution.py:252
  108.1 3.9 %collective-permute-start.24 = (f32[1,6144]{1,0:T(1,128)S(1)}, f32[1,6144]{1,0:T(1,128)S(1)}, u32[]{:S(2)}, u32[]{:S(2)}) collective-permute-start(f32[1,6144]{1,0:T(1,128)S(1)} %pad_maximum_fusion.2), channel_id=1, source_target_pairs={{0,4},{4,0},{8,12},{12,8},{16,20},{20,16},{24,28},{28,24},{1,5},{5... | collective-permute-start | bytes 73736 | tf_op jit(solution)/shard_map/ppermute | solution.py:252
